TPU v7x, 32 devices: a whole 2x2x4 slice. The times are simulated.
32 devices in a mesh: gx: 2 (over core), gy: 4 (over y, x), gz: 4 (over z).
Axes of the slice: x: 2, y: 2, z: 4, core: 2. Of those that a mesh axis runs over, the one named last changes fastest.
Arguments:
- places: float32 [3, 12, 4, 24, 128], P(None, 'gx', 'gy', 'gz'), may hold values from 0.45 to 8.35, as said below
- velocity: float32 [3, 12, 4, 24, 128], P(None, 'gx', 'gy', 'gz'), may hold values from -6 to 6
- forces_old: float32 [3, 12, 4, 24, 128], P(None, 'gx', 'gy', 'gz'), may hold values from -48 to 48
- counts: int32 [12, 4, 24], P('gx', 'gy', 'gz'), may hold values from 16 to 120, as said below
- mig_atom: int32 [2, 4, 4, 16], P('gx', 'gy', 'gz'), may hold values from 0 to 4607, as said below
- mig_face: int32 [2, 4, 4, 16], P('gx', 'gy', 'gz'), may hold values from 0 to 5, as said below
Outputs:
- new_places: float32 [3, 12, 4, 24, 128], P(None, 'gx', 'gy', 'gz')
- new_velocity: float32 [3, 12, 4, 24, 128], P(None, 'gx', 'gy', 'gz')
- new_forces: float32 [3, 12, 4, 24, 128], P(None, 'gx', 'gy', 'gz')
Inputs may be any that keep to these rules, and one draw needn't show every extreme that they name: `places`: within a cell and between neighbouring cells, any two slots lie at least 0.7 apart. `counts`: some cell holds exactly 120 atoms. `mig_atom`: each device's 16 entries name occupied slots of 16 distinct cells. `mig_face`: each entry's cell lies on the named face of its device's block.
All inputs are finite; a program needn't handle non-finite values.
Results may differ from a plain program's by a relative error of at most 0.0003.
Values sent between devices are 32-bit elements; how exact they have to be, the bound alone decides.
No kernel may reach another device: no remote copies, remote signals or barrier semaphores. Data moves between devices by JAX's collectives and lax.ppermute only.
A program may use at most 64 MiB of HBM per device.

v0:
```python
import functools

import jax
import jax.numpy as jnp
from jax import lax
from jax.experimental import pallas as pl
from jax.experimental.pallas import tpu as pltpu
from jax.sharding import PartitionSpec as P

step_size = 0.005
cut_radius = 2.5
spacing = 1.1
edge_force = 24.0 * (2.0 * cut_radius ** (-13) - cut_radius ** (-7))

FAR = 1.0e6
NEAR = 1.0e5
MARGIN = 1.0e-3
ROWS = 32
GROUP = 8
ARRIVALS = 4
SHORT = 3
CHUNKS = 6
PART = 32
APART = 1.0e-2
COMBOS = [(dx, dy, dz) for dx in (-1, 0, 1) for dy in (-1, 0, 1) for dz in (-1, 0, 1)]
NEIGHBOURS = sorted(
    (c for c in COMBOS if c != (0, 0, 0)),
    key=lambda c: abs(c[0]) + abs(c[1]) + 2 * abs(c[2]),
)
BATCHES = 7


def cell_sides(slot_count):
    return (4.0 * spacing, 4.0 * spacing, spacing * (slot_count // 16))


def take(tile, index):
    return jnp.take_along_axis(tile, index, axis=1, mode="promise_in_bounds")


def rows_of(ref, c, x, size_z, slots):
    sub = lax.broadcasted_iota(jnp.int32, (size_z, slots), 0)
    tile = jnp.broadcast_to(ref[c, x, 0], (size_z, slots))
    for z in range(1, size_z):
        tile = jnp.where(sub == z, ref[c, x, z], tile)
    return tile


def pack_kernel(
    count_ref, atom_ref, face_ref, place_ref, velocity_ref, force_ref,
    slab_ref, first_ref, last_ref, half_ref,
):
    _, size_x, size_z, _, slots = place_ref.shape
    sides = cell_sides(slots)
    sub = lax.broadcasted_iota(jnp.int32, (size_z, slots), 0)
    lane = lax.broadcasted_iota(jnp.int32, (size_z, slots), 1)
    letter = slots - 6
    entries = atom_ref.shape[0]
    atoms = [atom_ref[e] for e in range(entries)]
    faces = [face_ref[e] for e in range(entries)]
    for x in range(size_x):
        count = jnp.zeros((size_z, slots), jnp.int32)
        for z in range(size_z):
            count = jnp.where(sub == z, count_ref[x, 0, z], count)
        first_atom = (x * size_z + sub) * slots
        leaving = jnp.full((size_z, slots), -1, jnp.int32)
        face = jnp.full((size_z, slots), -8, jnp.int32)
        for e in range(entries):
            offset = atoms[e] - first_atom
            here = (offset >= 0) & (offset < slots)
            leaving = jnp.where(here, offset, leaving)
            face = jnp.where(here, faces[e], face)
        any_leaves = leaving >= 0
        picked = jnp.maximum(leaving, 0)
        order = jnp.bitwise_xor(face, 1)
        axis_of = lax.shift_right_arithmetic(face, 1)
        sign = (2 * (face & 1) - 1).astype(jnp.float32)
        alive = (lane < count) & (lane != leaving)
        letter_lane = any_leaves & (lane == letter + order)
        speed_lane = lane == letter - 1
        letters = jnp.full((size_z, slots), FAR, jnp.float32)
        for c in range(3):
            half = rows_of(velocity_ref, c, x, size_z, slots) + (
                0.5 * step_size * rows_of(force_ref, c, x, size_z, slots)
            )
            drifted = rows_of(place_ref, c, x, size_z, slots) + step_size * half
            half_ref[c, x] = half
            moved = take(drifted, picked) - jnp.where(axis_of == c, sign * sides[c], 0.0)
            tile = jnp.where(alive, drifted, FAR)
            tile = jnp.where(letter_lane, moved, tile)
            tile = jnp.where(speed_lane, take(half, picked), tile)
            slab_ref[c, x] = tile
            first_ref[c, x] = tile[:1]
            last_ref[c, x] = tile[size_z - 1 :]
            letters = jnp.where(any_leaves & (lane == letter + order - 8 * c), moved, letters)
        slab_ref[3, x] = letters
        first_ref[3, x] = letters[:1]
        last_ref[3, x] = letters[size_z - 1 :]


def append_batch(batch, scanned, chunks, filled):
    rows, slots = filled.shape
    lane = lax.broadcasted_iota(jnp.int32, (rows, slots), 1)
    rank = (lane - filled) & (slots - 1)
    packed, start = scanned[0]
    place_shift = jnp.zeros((rows, slots), jnp.int32)
    local = rank
    picks = []
    for s in range(1, len(batch)):
        packed = packed | lax.shift_left(scanned[s][0], 8 * s)
        later = rank >= start
        picks.append(later)
        place_shift = jnp.where(later, 8 * s, place_shift)
        local = jnp.where(later, rank - start, local)
        start = start + scanned[s][1]
    position = jnp.zeros((rows, slots), jnp.int32)
    step = slots // 2
    while step >= 1:
        probe = take(packed, position + (step - 1))
        probe = lax.shift_right_logical(probe, place_shift) & 255
        position = jnp.where(probe <= local, position + step, position)
        step //= 2
    moved = []
    for c in range(3):
        value = take(batch[0][c], position)
        for s in range(1, len(batch)):
            value = jnp.where(picks[s - 1], take(batch[s][c], position), value)
        moved.append(value)
    chunk_id = lax.shift_right_logical(filled + rank, slots.bit_length() - 1)
    chunk_id = jnp.where(rank < start, chunk_id, -1)
    for k in range(len(chunks)):
        chosen = chunk_id == k
        chunks[k] = [jnp.where(chosen, moved[c], chunks[k][c]) for c in range(3)]
    return chunks, filled + start, start


def pair_force(own, other):
    total = [None, None, None]
    for row in other:
        delta = [own[c] - row[c] for c in range(3)]
        square = delta[0] * delta[0] + delta[1] * delta[1] + delta[2] * delta[2]
        root = lax.rsqrt(square)
        inverse = root * root
        fourth = inverse * inverse
        sixth = fourth * inverse
        strength = (48.0 * sixth - 24.0) * (fourth * fourth) - edge_force * root
        inside = (square < cut_radius * cut_radius) & (square > APART)
        strength = jnp.where(inside, strength, 0.0)
        for c in range(3):
            part = delta[c] * strength
            total[c] = part if total[c] is None else total[c] + part
    return total


def row_sums(found):
    return [jnp.sum(f, axis=1, keepdims=True) for f in found]


def force_kernel(
    count_ref,
    own_ref,
    low_ref,
    high_ref,
    far_low_ref,
    far_high_ref,
    half_ref,
    out_place_ref,
    out_velocity_ref,
    out_force_ref,
    comb,
    reach,
    cand,
    own_t,
    force_t,
    arrival_force,
    chunk_count,
    items,
    arrivals,
):
    _, ext_x, ext_z, slots = own_ref.shape
    size_x, size_z = ext_x - 2, ext_z - 2
    sides = cell_sides(slots)
    letter = slots - 6
    sub = lax.broadcasted_iota(jnp.int32, (ext_z, slots), 0)
    lane = lax.broadcasted_iota(jnp.int32, (ext_z, slots), 1)
    inner = (sub >= 1) & (sub <= size_z)
    far_tile = jnp.full((ext_z, slots), FAR, jnp.float32)
    planes = [low_ref, own_ref, high_ref]

    from_z_low = (lane == letter + 4) & (sub > 0)
    from_z_high = (lane == letter + 5) & (sub < ext_z - 1)
    for x in range(ext_x):
        for y in range(3):
            for c in range(3):
                tile = planes[y][c, x]
                out = jnp.where(lane < letter - 1, tile, FAR)
                if x > 0:
                    out = jnp.where(lane == letter, planes[y][c, x - 1], out)
                if x < ext_x - 1:
                    out = jnp.where(lane == letter + 1, planes[y][c, x + 1], out)
                below = planes[y - 1][c, x] if y > 0 else pltpu.roll(far_low_ref[x], 8 * c, 1)
                above = planes[y + 1][c, x] if y < 2 else pltpu.roll(far_high_ref[x], 8 * c, 1)
                out = jnp.where(lane == letter + 2, below, out)
                out = jnp.where(lane == letter + 3, above, out)
                out = jnp.where(from_z_low, pltpu.roll(tile, 1, 0), out)
                out = jnp.where(from_z_high, pltpu.roll(tile, ext_z - 1, 0), out)
                comb[c, x, y] = out

    lower, upper = [], []
    for c in range(3):
        low_tile = jnp.full((ext_z, slots), FAR, jnp.float32)
        high_tile = jnp.full((ext_z, slots), -FAR, jnp.float32)
        for x in range(1, size_x + 1):
            tile = own_ref[c, x]
            real = inner & (lane < letter - 1) & (tile < NEAR)
            low_tile = jnp.minimum(low_tile, jnp.where(real, tile, FAR))
            high_tile = jnp.maximum(high_tile, jnp.where(real, tile, -FAR))
        lower.append(jnp.min(low_tile, axis=(0, 1), keepdims=True) - (cut_radius + MARGIN))
        upper.append(jnp.max(high_tile, axis=(0, 1), keepdims=True) + (cut_radius + MARGIN))

    for x in range(ext_x):
        for y in range(3):
            for dz in (-1, 0, 1):
                tiles = [comb[c, x, y] for c in range(3)]
                if dz:
                    tiles = [pltpu.roll(t, (-dz) % ext_z, 0) for t in tiles]
                    tiles[2] = tiles[2] + dz * sides[2]
                usable = inner
                if dz:
                    usable = usable & ((tiles[2] > lower[2]) if dz < 0 else (tiles[2] < upper[2]))
                if y != 1:
                    tiles[1] = tiles[1] + (y - 1) * sides[1]
                    usable = usable & ((tiles[1] > lower[1]) if y == 0 else (tiles[1] < upper[1]))
                reach[dz + 1, 0, x, y] = jnp.where(usable, tiles[0], FAR)
                reach[dz + 1, 1, x, y] = tiles[1]
                reach[dz + 1, 2, x, y] = tiles[2]

    row_id = lax.broadcasted_iota(jnp.int32, (slots, 2 * slots), 0)
    col_id = lax.broadcasted_iota(jnp.int32, (slots, 2 * slots), 1)
    weights = jnp.where(row_id <= col_id, 1.0, 0.0).astype(jnp.bfloat16)
    excess = jnp.full((ext_z, slots), -1, jnp.int32)
    counts = []
    for x in range(size_x):
        count = jnp.zeros((ext_z, slots), jnp.int32)
        for z in range(size_z):
            count = jnp.where(sub == z + 1, count_ref[x, 0, z], count)
        counts.append(count)

    chunk_tiles = []
    for x in range(size_x):
        center = [comb[c, x + 1, 1] for c in range(3)]
        sources = [(inner & (lane >= letter) & (center[0] < NEAR), center)]
        for dx, dy, dz in NEIGHBOURS:
            tiles = [reach[dz + 1, c, x + 1 + dx, 1 + dy] for c in range(3)]
            real = tiles[0] < NEAR
            if dx:
                tiles[0] = tiles[0] + dx * sides[0]
                real = real & ((tiles[0] > lower[0]) if dx < 0 else (tiles[0] < upper[0]))
            sources.append((real, tiles))
        masks = jnp.concatenate([jnp.where(m, 1.0, 0.0) for m, _ in sources], axis=0)
        scanned = jnp.dot(
            masks.astype(jnp.bfloat16), weights, preferred_element_type=jnp.float32
        ).astype(jnp.int32)
        split = []
        for s in range(len(sources)):
            part = scanned[ext_z * s : ext_z * (s + 1)]
            split.append((part[:, :slots], part[:, slots:]))
        chunks = [[jnp.where(lane < counts[x], t, FAR) for t in center]]
        chunks += [[far_tile] * 3 for _ in range(CHUNKS - 1)]
        filled = counts[x]
        for batch in range(BATCHES):
            ids = range(batch, len(sources), BATCHES)
            chunks, filled, added = append_batch(
                [sources[s][1] for s in ids], [split[s] for s in ids], chunks, filled
            )
            excess = jnp.maximum(excess, added - slots)
        excess = jnp.maximum(excess, filled - CHUNKS * slots)
        for k in range(CHUNKS):
            for c in range(3):
                cand[x, k, c] = chunks[k][c]
        chunk_tiles.append(lax.shift_right_logical(filled + (slots - 1), slots.bit_length() - 1))

    overflow = jnp.max(excess.astype(jnp.float32)) > 0.0
    longest = functools.reduce(jnp.maximum, chunk_tiles)
    longest = jnp.max(jnp.where(inner, longest, 0).astype(jnp.float32)) > SHORT
    position = 0
    for x in range(size_x):
        for z in range(size_z):
            chunk_count[x, z] = jnp.where(overflow, len(COMBOS), chunk_tiles[x][z + 1, 0])
            code = x * 256 + z * 16
            for block in range(slots // 8):
                items[position + block] = code + block
            position = position + lax.shift_right_logical(count_ref[x, 0, z] + 7, 3)
    item_steps = lax.div(position + (GROUP - 1), GROUP)
    for extra in range(GROUP):
        items[position + extra] = slots // 8 - 1
    position = 0
    for x in range(size_x):
        arrived = jnp.zeros((ext_z, slots), jnp.float32)
        for o in range(6):
            arrived = jnp.where(lane == letter + o, float(2**o), arrived)
        arrived = jnp.where(comb[0, x + 1, 1] < NEAR, arrived, 0.0)
        arrived = jnp.sum(arrived, axis=1, keepdims=True).astype(jnp.int32)
        for z in range(size_z):
            bits = arrived[z + 1, 0]
            for o in range(6):
                arrivals[position] = x * 256 + z * 16 + o
                position = position + (lax.shift_right_logical(bits, o) & 1)
    arrival_steps = lax.div(position + (ARRIVALS - 1), ARRIVALS)
    for extra in range(ARRIVALS):
        arrivals[position + extra] = 7

    @pl.when(overflow)
    def _():
        for k, (dx, dy, dz) in enumerate(COMBOS):
            for x in range(size_x):
                for c, step in enumerate((dx, dy, dz)):
                    tile = comb[c, x + 1 + dx, 1 + dy]
                    if dz:
                        tile = pltpu.roll(tile, (-dz) % ext_z, 0)
                    cand[x, k, c] = tile + step * sides[c]

    for x in range(size_x):
        parts = []
        rest = [comb[c, x + 1, 1] for c in range(3)]
        for _ in range(3):
            rounded = [r.astype(jnp.bfloat16).astype(jnp.float32) for r in rest]
            rest = [r - h for r, h in zip(rest, rounded)]
            parts += rounded + [jnp.zeros((PART - 3 * ext_z, slots), jnp.float32)]
        parts.append(jnp.zeros((slots - 3 * PART, slots), jnp.float32))
        own_t[x] = jnp.concatenate(parts, axis=0).T
        force_t[x] = jnp.zeros((slots, slots), jnp.float32)

    for x in range(size_x):
        for c in range(3):
            arrival_force[x, c] = jnp.zeros((ext_z, slots), jnp.float32)

    row_id = lax.broadcasted_iota(jnp.int32, (slots, 3 * slots), 0)
    col_id = lax.broadcasted_iota(jnp.int32, (slots, 3 * slots), 1)
    of_axis = lax.shift_right_logical(row_id & (PART - 1), 3)
    spread = (of_axis == lax.shift_right_logical(col_id, 7)) & (row_id < 3 * PART)
    spread = jnp.where(spread, 1.0, 0.0).astype(jnp.bfloat16)
    summing = jnp.ones((2 * slots, slots), jnp.bfloat16)

    def each_group(group, carry):
        work, held = [], []
        for g in range(GROUP):
            code = items[group * GROUP + g]
            x = lax.shift_right_logical(code, 8)
            z = lax.shift_right_logical(code, 4) & 15
            rows = pl.ds(pl.multiple_of((code & 15) * 8, 8), 8)
            held.append(jnp.where((lane & 7) == z + 1, own_t[x, rows, :], 0.0))
            work.append((x, z, rows))
        columns = jnp.dot(
            jnp.concatenate(held, axis=0).astype(jnp.bfloat16),
            spread,
            preferred_element_type=jnp.float32,
        )
        found = []
        for g, (x, z, _) in enumerate(work):
            own = [columns[8 * g : 8 * g + 8, c * slots : (c + 1) * slots] for c in range(3)]
            other = [
                [cand[x, k, c, pl.ds(z + 1, 1), :] for c in range(3)] for k in range(SHORT)
            ]
            found += pair_force(own, other)
        found = jnp.concatenate(found, axis=0)
        rounded = found.astype(jnp.bfloat16)
        rest = (found - rounded.astype(jnp.float32)).astype(jnp.bfloat16)
        found = jnp.dot(
            jnp.concatenate([rounded, rest], axis=1), summing, preferred_element_type=jnp.float32
        )
        for g, (x, z, rows) in enumerate(work):
            result = force_t[x, rows, :]
            for c in range(3):
                start = (3 * g + c) * 8
                result = jnp.where(lane == c * ext_z + z + 1, found[start : start + 8], result)
            force_t[x, rows, :] = result
        return carry

    lax.fori_loop(0, item_steps, each_group, 0)

    def each_arrival(group, carry):
        work = []
        for g in range(ARRIVALS):
            code = arrivals[group * ARRIVALS + g]
            x = lax.shift_right_logical(code, 8)
            z = lax.shift_right_logical(code, 4) & 15
            slot = letter + (code & 15)
            pick = jnp.full((ext_z, slots), slot & (slots - 1), jnp.int32)
            own = []
            for c in range(3):
                row = comb[c, x + 1, 1, pl.ds(z + 1, 1), :]
                own.append(take(jnp.broadcast_to(row, (ext_z, slots)), pick))
            away = sub - (z + 1)
            rise = away.astype(jnp.float32) * sides[2]
            beside = jnp.abs(away) <= 1
            other = []
            for dx in (-1, 0, 1):
                for dy in (-1, 0, 1):
                    tiles = [comb[c, x + 1 + dx, 1 + dy] for c in range(3)]
                    tiles[0] = jnp.where(beside, tiles[0], FAR)
                    tiles[0] = tiles[0] + dx * sides[0] if dx else tiles[0]
                    tiles[1] = tiles[1] + dy * sides[1] if dy else tiles[1]
                    tiles[2] = tiles[2] + rise
                    other.append(tiles)
            found = row_sums(pair_force(own, other))
            found = [jnp.sum(f, axis=0, keepdims=True) for f in found]
            work.append((x, (sub == z + 1) & (lane == slot), found))
        for x, spot, found in work:
            for c in range(3):
                arrival_force[x, c] = jnp.where(spot, found[c], arrival_force[x, c])
        return carry

    lax.fori_loop(0, arrival_steps, each_arrival, 0)

    lane_rows = lax.broadcasted_iota(jnp.int32, (ROWS, slots), 1)
    row_shift = ROWS.bit_length() - 1

    @pl.when(overflow | longest)
    def _():
        def each_x(x, carry):
            for z in range(size_z):
                picks = [c * ext_z + z + 1 for c in range(3)]
                blocks = lax.shift_right_logical(count_ref[x, 0, z] + (ROWS - 1), row_shift)

                def each_chunk(k, chunk_carry):
                    def each_block(block, block_carry):
                        rows = pl.ds(pl.multiple_of(block * ROWS, ROWS), ROWS)
                        held = own_t[x, rows, :]
                        own = []
                        for p in picks:
                            parts = [held[:, p + PART * i : p + PART * i + 1] for i in range(3)]
                            own.append(parts[0] + parts[1] + parts[2])
                        chunk = [cand[x, k, c, z + 1 : z + 2, :] for c in range(3)]
                        found = row_sums(pair_force(own, [chunk]))
                        result = force_t[x, rows, :]
                        for c in range(3):
                            result = jnp.where(lane_rows == picks[c], result + found[c], result)
                        force_t[x, rows, :] = result
                        return block_carry

                    return lax.fori_loop(0, blocks, each_block, chunk_carry)

                lax.fori_loop(SHORT, chunk_count[x, z], each_chunk, 0)
            return carry

        lax.fori_loop(0, size_x, each_x, 0)

    speed = jnp.full((ext_z, slots), letter - 1, jnp.int32)
    for x in range(size_x):
        turned = force_t[x].T
        count = counts[x]
        base = comb[0, x + 1, 1]
        filled = count
        index = lane
        for o in range(6):
            valid = take(base, jnp.full((ext_z, slots), letter + o, jnp.int32)) < NEAR
            index = jnp.where(valid & (lane == filled), letter + o, index)
            filled = filled + jnp.where(valid, 1, 0)
        placed = take(base, index)
        alive = (lane < filled) & (placed < NEAR)
        for c in range(3):
            half = half_ref[c, x]
            blank = jnp.zeros((1, slots), jnp.float32)
            half = jnp.concatenate([blank, half, blank], axis=0)
            tile = own_ref[c, x + 1]
            sent = [
                own_ref[c, x],
                own_ref[c, x + 2],
                low_ref[c, x + 1],
                high_ref[c, x + 1],
                pltpu.roll(tile, 1, 0),
                pltpu.roll(tile, ext_z - 1, 0),
            ]
            for o in range(6):
                half = jnp.where(lane == letter + o, take(sent[o], speed), half)
            where_to = placed if c == 0 else take(comb[c, x + 1, 1], index)
            force = turned[c * ext_z : (c + 1) * ext_z]
            force = jnp.where(lane >= letter, arrival_force[x, c], force)
            force = jnp.where(alive, take(force, index), 0.0)
            half = take(half, index) + 0.5 * step_size * force
            where_to = jnp.where(alive, where_to, 0.0)
            half = jnp.where(alive, half, 0.0)
            for z in range(size_z):
                out_place_ref[c, x, z] = where_to[z + 1 : z + 2]
                out_velocity_ref[c, x, z] = half[z + 1 : z + 2]
                out_force_ref[c, x, z] = force[z + 1 : z + 2]


def shifted(value, axis, steps):
    count = lax.axis_size(axis)
    return lax.ppermute(value, axis, [(i, (i + steps) % count) for i in range(count)])


def per_device(places, velocity, forces_old, counts, mig_atom, mig_face):
    size_x, size_y, size_z, slots = places.shape[1:]
    assert size_y == 1 and size_z == 6 and slots == 128 and size_x >= 2
    flat = (size_x, size_z, slots)
    swapped = [jnp.transpose(a, (0, 1, 3, 2, 4)) for a in (places, velocity, forces_old)]
    vmem = pl.BlockSpec(memory_space=pltpu.VMEM)
    smem = pl.BlockSpec(memory_space=pltpu.SMEM)
    slab, first, last, half = pl.pallas_call(
        pack_kernel,
        out_shape=[
            jax.ShapeDtypeStruct((4,) + flat, jnp.float32),
            jax.ShapeDtypeStruct((4, size_x, 1, slots), jnp.float32),
            jax.ShapeDtypeStruct((4, size_x, 1, slots), jnp.float32),
            jax.ShapeDtypeStruct((3,) + flat, jnp.float32),
        ],
        in_specs=[smem] * 3 + [vmem] * 3,
        out_specs=[vmem] * 4,
    )(counts, mig_atom.reshape(-1), mig_face.reshape(-1), *swapped)

    from_low = shifted(last, "gz", 1)
    from_high = shifted(first, "gz", -1)
    slab = jnp.concatenate([from_low, slab, from_high], axis=2)
    if lax.axis_size("gx") == 2:
        both = shifted(jnp.concatenate([slab[:, :1], slab[:, size_x - 1 :]], axis=1), "gx", 1)
        from_low, from_high = both[:, 1:], both[:, :1]
    else:
        from_low = shifted(slab[:, size_x - 1 :], "gx", 1)
        from_high = shifted(slab[:, :1], "gx", -1)
    slab = jnp.concatenate([from_low, slab, from_high], axis=1)
    own, letters = slab[:3], slab[3]
    low = shifted(own, "gy", 1)
    high = shifted(own, "gy", -1)
    far_low = shifted(letters, "gy", 2)
    far_high = far_low if lax.axis_size("gy") == 4 else shifted(letters, "gy", -2)

    ext_x, ext_z = size_x + 2, size_z + 2
    outs = pl.pallas_call(
        force_kernel,
        out_shape=[jax.ShapeDtypeStruct(swapped[0].shape, jnp.float32)] * 3,
        in_specs=[smem] + [vmem] * 6,
        out_specs=[vmem] * 3,
        scratch_shapes=[
            pltpu.VMEM((3, ext_x, 3, ext_z, slots), jnp.float32),
            pltpu.VMEM((3, 3, ext_x, 3, ext_z, slots), jnp.float32),
            pltpu.VMEM((size_x, len(COMBOS), 3, ext_z, slots), jnp.float32),
            pltpu.VMEM((size_x, slots, slots), jnp.float32),
            pltpu.VMEM((size_x, slots, slots), jnp.float32),
            pltpu.VMEM((size_x, 3, ext_z, slots), jnp.float32),
            pltpu.SMEM((size_x, size_z), jnp.int32),
            pltpu.SMEM((size_x * size_z * (slots // 8) + GROUP,), jnp.int32),
            pltpu.SMEM((size_x * size_z * 6 + ARRIVALS,), jnp.int32),
        ],
        compiler_params=pltpu.CompilerParams(vmem_limit_bytes=24 * 1024 * 1024),
    )(counts, own, low, high, far_low, far_high, half)
    return tuple(jnp.transpose(o, (0, 1, 3, 2, 4)) for o in outs)


def solution(mesh):
    block = P(None, "gx", "gy", "gz", None)
    return jax.shard_map(
        per_device,
        mesh=mesh,
        in_specs=(
            block,
            block,
            block,
            P("gx", "gy", "gz"),
            P("gx", "gy", "gz", None),
            P("gx", "gy", "gz", None),
        ),
        out_specs=(block, block, block),
        check_vma=False,
    )
```

profile of v0, /device:TPU:24, one launch (start us, length us, event | category | flops | bytes accessed | tf_op | source)
XLA Modules:
  0.0 37.5 jit_solution(13039255135260597441)
XLA Ops:
  0.6 1.8 %shard_map.85 = (f32[4,6,6,128]{3,2,1,0:T(8,128)}, f32[4,6,1,128]{3,2,1,0:T(1,128)}, f32[4,6,1,128]{3,2,1,0:T(1,128)}, f32[3,6,6,128]{3,2,1,0:T(8,128)}) custom-call(s32[6,1,6]{2,1,0:T(1,128)} %count_ref.3, s32[16]{0:T(128)} %bitcast.13, s32[16]{0:T(128)} %bitcast.14, f32[3,6,6,1,128]{4,3,2,1,0:T(1,128)} %bitcast.10, f32[3,6,6,1,128]{4,3,2,1,0:T(1,128)} %bitcast.11, ...), custom_call_target="tpu_custom_call" | custom-call | tf_op jit(solution)/shard_map/pallas_call | solution.py:502
  2.4 0.0 collective-permute-start
  2.4 2.0 %collective-permute-start.1 = (f32[4,6,1,128]{3,2,1,0:T(1,128)}, f32[4,6,1,128]{3,2,1,0:T(1,128)S(1)}, u32[]{:S(2)}, u32[]{:S(2)}) collective-permute-start(f32[4,6,1,128]{3,2,1,0:T(1,128)} %get-tuple-element.12), channel_id=1, source_target_pairs={{0,3},{1,0},{2,1},{3,2},{4,7},{5,4},{6,5},{7,6},{8,11},{9,8},{10,9... | collective-permute-start | bytes 36872 | tf_op jit(solution)/shard_map/ppermute | solution.py:492
  4.5 1.9 %collective-permute-done = f32[4,6,1,128]{3,2,1,0:T(1,128)S(1)} collective-permute-done((f32[4,6,1,128]{3,2,1,0:T(1,128)}, f32[4,6,1,128]{3,2,1,0:T(1,128)S(1)}, u32[]{:S(2)}, u32[]{:S(2)}) %collective-permute-start) | collective-permute-done | bytes 12320 | tf_op jit(solution)/shard_map/ppermute | solution.py:492
  6.3 1.9 %collective-permute-done.1 = f32[4,6,1,128]{3,2,1,0:T(1,128)S(1)} collective-permute-done((f32[4,6,1,128]{3,2,1,0:T(1,128)}, f32[4,6,1,128]{3,2,1,0:T(1,128)S(1)}, u32[]{:S(2)}, u32[]{:S(2)}) %collective-permute-start.1) | collective-permute-done | bytes 12320 | tf_op jit(solution)/shard_map/ppermute | solution.py:492
  8.2 0.0 copy-start.2
  8.2 0.8 %fusion = f32[4,2,8,128]{3,2,1,0:T(8,128)S(1)} fusion(f32[4,6,1,128]{3,2,1,0:T(1,128)S(1)} %collective-permute-done.1, f32[4,6,6,128]{3,2,1,0:T(8,128)} %get-tuple-element.11, f32[4,6,1,128]{3,2,1,0:T(1,128)S(1)} %collective-permute-done), kind=kLoop, calls=%fused_computation.3 | loop fusion | flops 106496 | bytes 131072 | tf_op jit(solution)/shard_map/concatenate | solution.py:518
  9.0 0.1 collective-permute-start.2
  9.1 1.2 %collective-permute-done.2 = f32[4,2,8,128]{3,2,1,0:T(8,128)S(1)} collective-permute-done((f32[4,2,8,128]{3,2,1,0:T(8,128)S(1)}, f32[4,2,8,128]{3,2,1,0:T(8,128)S(1)}, u32[]{:S(2)}, u32[]{:S(2)}) %collective-permute-start.2) | collective-permute-done | bytes 32800 | tf_op jit(solution)/shard_map/ppermute | solution.py:492
  10.3 0.0 copy-done.2
  10.4 0.0 copy-start
  10.4 2.7 %collective-permute-start.4 = (f32[3,8,8,128]{3,2,1,0:T(8,128)S(1)}, f32[3,8,8,128]{3,2,1,0:T(8,128)S(1)}, u32[]{:S(2)}, u32[]{:S(2)}) collective-permute-start(f32[3,8,8,128]{3,2,1,0:T(8,128)S(1)} %slice.26.own_ref), channel_id=1, source_target_pairs={{0,12},{4,0},{8,4},{12,8},{1,13},{5,1},{9,5},{13,9},{2,14},{6,2},{... | collective-permute-start | bytes 294920 | tf_op jit(solution)/shard_map/ppermute | solution.py:492
  13.1 0.0 collective-permute-start.3
  13.1 0.0 copy-start.1
  13.1 1.2 %collective-permute-start.5 = (f32[8,8,128]{2,1,0:T(8,128)S(1)}, f32[8,8,128]{2,1,0:T(8,128)S(1)}, u32[]{:S(2)}, u32[]{:S(2)}) collective-permute-start(f32[8,8,128]{2,1,0:T(8,128)S(1)} %maximum_bitcast_fusion), channel_id=1, source_target_pairs={{0,8},{4,12},{8,0},{12,4},{1,9},{5,13},{9,1},{13,5},{2,10},{6,14},... | collective-permute-start | bytes 98312 | tf_op jit(solution)/shard_map/ppermute | solution.py:492
  14.2 4.6 %collective-permute-done.5.far_low_ref.far_high_ref = f32[8,8,128]{2,1,0:T(8,128)S(1)} collective-permute-done((f32[8,8,128]{2,1,0:T(8,128)S(1)}, f32[8,8,128]{2,1,0:T(8,128)S(1)}, u32[]{:S(2)}, u32[]{:S(2)}) %collective-permute-start.5) | collective-permute-done | bytes 32800 | tf_op jit(solution)/shard_map/ppermute | solution.py:492
  18.9 0.0 collective-permute-done.4.high_ref
  18.9 0.0 collective-permute-done.3.low_ref
  18.9 0.0 copy-done
  18.9 0.0 copy-done.1
  18.9 18.6 %shard_map.86 = (f32[3,6,6,1,128]{4,3,2,1,0:T(1,128)}, f32[3,6,6,1,128]{4,3,2,1,0:T(1,128)}, f32[3,6,6,1,128]{4,3,2,1,0:T(1,128)}) custom-call(s32[6,1,6]{2,1,0:T(1,128)S(1)} %copy-done.1, f32[3,8,8,128]{3,2,1,0:T(8,128)S(1)} %slice.26.own_ref, f32[3,8,8,128]{3,2,1,0:T(8,128)S(1)} %collective-permute-done.3.low_ref, ...), custom_call_target="tpu_custom_call" | custom-call | tf_op jit(solution)/shard_map/pallas_call | solution.py:531
  (4 shorter events, 0.1 us)
Async XLA Ops:
  2.4 3.9 %collective-permute-start = (f32[4,6,1,128]{3,2,1,0:T(1,128)}, f32[4,6,1,128]{3,2,1,0:T(1,128)S(1)}, u32[]{:S(2)}, u32[]{:S(2)}) collective-permute-start(f32[4,6,1,128]{3,2,1,0:T(1,128)} %get-tuple-element.10), channel_id=1, source_target_pairs={{0,1},{1,2},{2,3},{3,0},{4,5},{5,6},{6,7},{7,4},{8,9},{9,10},{10,1... | collective-permute-start | bytes 36872 | tf_op jit(solution)/shard_map/ppermute | solution.py:492
  2.4 5.8 %collective-permute-start.1 = (f32[4,6,1,128]{3,2,1,0:T(1,128)}, f32[4,6,1,128]{3,2,1,0:T(1,128)S(1)}, u32[]{:S(2)}, u32[]{:S(2)}) collective-permute-start(f32[4,6,1,128]{3,2,1,0:T(1,128)} %get-tuple-element.12), channel_id=1, source_target_pairs={{0,3},{1,0},{2,1},{3,2},{4,7},{5,4},{6,5},{7,6},{8,11},{9,8},{10,9... | collective-permute-start | bytes 36872 | tf_op jit(solution)/shard_map/ppermute | solution.py:492
  8.2 2.1 %copy-start.2 = (f32[4,6,6,128]{3,2,1,0:T(8,128)S(1)}, f32[4,6,6,128]{3,2,1,0:T(8,128)}, u32[]{:S(2)}) copy-start(f32[4,6,6,128]{3,2,1,0:T(8,128)} %get-tuple-element.11) | copy-start | bytes 221188
  9.0 1.3 %collective-permute-start.2 = (f32[4,2,8,128]{3,2,1,0:T(8,128)S(1)}, f32[4,2,8,128]{3,2,1,0:T(8,128)S(1)}, u32[]{:S(2)}, u32[]{:S(2)}) collective-permute-start(f32[4,2,8,128]{3,2,1,0:T(8,128)S(1)} %fusion), channel_id=1, source_target_pairs={{0,16},{16,0},{1,17},{17,1},{2,18},{18,2},{3,19},{19,3},{4,20},{20... | collective-permute-start | bytes 98312 | tf_op jit(solution)/shard_map/ppermute | solution.py:492
  10.4 8.5 %copy-start = (f32[3,6,6,128]{3,2,1,0:T(8,128)S(1)}, f32[3,6,6,128]{3,2,1,0:T(8,128)}, u32[]{:S(2)}) copy-start(f32[3,6,6,128]{3,2,1,0:T(8,128)} %get-tuple-element.13.half_ref) | copy-start | bytes 165892
  10.4 8.5 %collective-permute-start.4 = (f32[3,8,8,128]{3,2,1,0:T(8,128)S(1)}, f32[3,8,8,128]{3,2,1,0:T(8,128)S(1)}, u32[]{:S(2)}, u32[]{:S(2)}) collective-permute-start(f32[3,8,8,128]{3,2,1,0:T(8,128)S(1)} %slice.26.own_ref), channel_id=1, source_target_pairs={{0,12},{4,0},{8,4},{12,8},{1,13},{5,1},{9,5},{13,9},{2,14},{6,2},{... | collective-permute-start | bytes 294920 | tf_op jit(solution)/shard_map/ppermute | solution.py:492
  13.1 5.8 %collective-permute-start.3 = (f32[3,8,8,128]{3,2,1,0:T(8,128)S(1)}, f32[3,8,8,128]{3,2,1,0:T(8,128)S(1)}, u32[]{:S(2)}, u32[]{:S(2)}) collective-permute-start(f32[3,8,8,128]{3,2,1,0:T(8,128)S(1)} %slice.26.own_ref), channel_id=1, source_target_pairs={{0,4},{4,8},{8,12},{12,0},{1,5},{5,9},{9,13},{13,1},{2,6},{6,10},{... | collective-permute-start | bytes 294920 | tf_op jit(solution)/shard_map/ppermute | solution.py:492
  13.1 5.8 %copy-start.1 = (s32[6,1,6]{2,1,0:T(1,128)S(1)}, s32[6,1,6]{2,1,0:T(1,128)}, u32[]{:S(2)}) copy-start(s32[6,1,6]{2,1,0:T(1,128)} %count_ref.3) | copy-start | bytes 436
  13.1 5.8 %collective-permute-start.5 = (f32[8,8,128]{2,1,0:T(8,128)S(1)}, f32[8,8,128]{2,1,0:T(8,128)S(1)}, u32[]{:S(2)}, u32[]{:S(2)}) collective-permute-start(f32[8,8,128]{2,1,0:T(8,128)S(1)} %maximum_bitcast_fusion), channel_id=1, source_target_pairs={{0,8},{4,12},{8,0},{12,4},{1,9},{5,13},{9,1},{13,5},{2,10},{6,14},... | collective-permute-start | bytes 98312 | tf_op jit(solution)/shard_map/ppermute | solution.py:492
where the time goes:
time: 37.3 us; the launch traced here: 37.5 us
  Pallas kernels  20.4 us (55%)
  waiting for transfers between devices  9.58 us (26%)
  starting transfers between devices  5.92 us (16%)
  other arithmetic  0.9 us (2%)
  between operations  0.69 us (2%)
    pallas_call x1, Pallas kernels, per_device(): pl.pallas_call(force_kernel, out_shape=[jax.ShapeDtypeStruct(swapped[0].s...  18.6 us
    ppermute x6, waiting for transfers between devices, shifted(): lax.ppermute(value, axis, [(i, (i + steps) % count) for i in range(count)])  9.58 us
    ppermute x6, starting transfers between devices, shifted(): lax.ppermute(value, axis, [(i, (i + steps) % count) for i in range(count)])  5.92 us
    pallas_call x1, Pallas kernels, per_device(): pl.pallas_call(pack_kernel, out_shape=[jax.ShapeDtypeStruct((4,) + flat,...  1.79 us
    concatenate x1, other arithmetic, per_device(): jnp.concatenate([slab[:, :1], slab[:, size_x - 1:]], axis=1)  0.85 us
  transfers between devices with their start and end apart: 6, of which 4 were waited for; matrix products, arithmetic and copies ran while one was open for 0% of the time, Pallas kernels for 0%

commit v1 on v0

--- a/solution.py
+++ b/solution.py
@@ -12,22 +12,25 @@
 spacing = 1.1
 edge_force = 24.0 * (2.0 * cut_radius ** (-13) - cut_radius ** (-7))
 
-FAR = 1.0e6
-NEAR = 1.0e5
+FAR = 24.0
+NEAR = 16.0
 MARGIN = 1.0e-3
-ROWS = 32
-GROUP = 8
+GROUP = 48
 ARRIVALS = 4
-SHORT = 3
+SHORT = 2
 CHUNKS = 6
+PLANE_CHUNKS = 3
 PART = 32
-APART = 1.0e-2
+APART = 0.25
 COMBOS = [(dx, dy, dz) for dx in (-1, 0, 1) for dy in (-1, 0, 1) for dz in (-1, 0, 1)]
-NEIGHBOURS = sorted(
-    (c for c in COMBOS if c != (0, 0, 0)),
-    key=lambda c: abs(c[0]) + abs(c[1]) + 2 * abs(c[2]),
-)
-BATCHES = 7
+
+
+def by_weight(combos):
+    return sorted(combos, key=lambda c: abs(c[0]) + abs(c[1]) + 2 * abs(c[2]))
+
+
+PLANE = by_weight(c for c in COMBOS if c[1] == 0 and c != (0, 0, 0))
+SIDES = by_weight(c for c in COMBOS if c[1] != 0)
 
 
 def cell_sides(slot_count):
@@ -139,13 +142,12 @@
     for row in other:
         delta = [own[c] - row[c] for c in range(3)]
         square = delta[0] * delta[0] + delta[1] * delta[1] + delta[2] * delta[2]
+        square = jnp.minimum(jnp.maximum(square, APART), cut_radius * cut_radius)
         root = lax.rsqrt(square)
         inverse = root * root
         fourth = inverse * inverse
         sixth = fourth * inverse
-        strength = (48.0 * sixth - 24.0) * (fourth * fourth) - edge_force * root
-        inside = (square < cut_radius * cut_radius) & (square > APART)
-        strength = jnp.where(inside, strength, 0.0)
+        strength = (sixth - 0.5) * (fourth * fourth) - (edge_force / 48.0) * root
         for c in range(3):
             part = delta[c] * strength
             total[c] = part if total[c] is None else total[c] + part
@@ -156,26 +158,217 @@
     return [jnp.sum(f, axis=1, keepdims=True) for f in found]
 
 
+def scan_weights(slots):
+    row_id = lax.broadcasted_iota(jnp.int32, (slots, 2 * slots), 0)
+    col_id = lax.broadcasted_iota(jnp.int32, (slots, 2 * slots), 1)
+    return jnp.where(row_id <= col_id, 1.0, 0.0).astype(jnp.bfloat16)
+
+
+def append_sources(sources, chunks, filled, excess, weights):
+    slots = weights.shape[0]
+    rows = filled.shape[0]
+    masks = jnp.concatenate([jnp.where(m, 1.0, 0.0) for m, _ in sources], axis=0)
+    scanned = jnp.dot(
+        masks.astype(jnp.bfloat16), weights, preferred_element_type=jnp.float32
+    ).astype(jnp.int32)
+    split = []
+    for s in range(len(sources)):
+        part = scanned[rows * s : rows * (s + 1)]
+        split.append((part[:, :slots], part[:, slots:]))
+    batches = -(-len(sources) // 4)
+    for batch in range(batches):
+        ids = range(batch, len(sources), batches)
+        chunks, filled, added = append_batch(
+            [sources[s][1] for s in ids], [split[s] for s in ids], chunks, filled
+        )
+        excess = jnp.maximum(excess, added - slots)
+    return chunks, filled, jnp.maximum(excess, filled - len(chunks) * slots)
+
+
+def sideways(tiles, dx, side, lower, upper):
+    real = tiles[0] < NEAR
+    if dx:
+        tiles = [tiles[0] + dx * side] + tiles[1:]
+        real = real & ((tiles[0] > lower) if dx < 0 else (tiles[0] < upper))
+    return real, tiles
+
+
+def pair_loop(items, steps, own_ref, cand, chunk_ids, force_ref, slots, ext_z):
+    lane = lax.broadcasted_iota(jnp.int32, (8, slots), 1)
+    shift = slots.bit_length() - 1
+    row_id = lax.broadcasted_iota(jnp.int32, (slots, 3 * slots), 0)
+    col_id = lax.broadcasted_iota(jnp.int32, (slots, 3 * slots), 1)
+    of_axis = lax.shift_right_logical(row_id & (PART - 1), 3)
+    spread = (of_axis == lax.shift_right_logical(col_id, shift)) & (row_id < 3 * PART)
+    spread = jnp.where(spread, 1.0, 0.0).astype(jnp.bfloat16)
+    row_id = lax.broadcasted_iota(jnp.int32, (3 * slots, slots), 0)
+    col_id = lax.broadcasted_iota(jnp.int32, (3 * slots, slots), 1) - 3 * PART
+    summing = (lax.shift_right_arithmetic(col_id, 3) == lax.shift_right_logical(row_id, shift))
+    summing = jnp.where(summing, 1.0, 0.0).astype(jnp.bfloat16)
+    summing = jnp.concatenate([summing, summing], axis=0)
+
+    def each_group(group, carry):
+        work, held = [], []
+        for g in range(GROUP):
+            code = items[group * GROUP + g]
+            x = lax.shift_right_logical(code, 8) & 15
+            z = lax.shift_right_logical(code, 4) & 15
+            first = lax.shift_right_logical(code, 12)
+            rows = pl.ds(pl.multiple_of((code & 15) * 8, 8), 8)
+            mask = (lane & 7) == z + 1
+            held.append(jnp.where(mask, own_ref[x, rows, :], 0.0))
+            work.append((x, z, first, rows, mask))
+        columns = jnp.dot(
+            jnp.concatenate(held, axis=0).astype(jnp.bfloat16),
+            spread,
+            preferred_element_type=jnp.float32,
+        )
+        found = []
+        for g, (x, z, first, _, _) in enumerate(work):
+            own = [columns[8 * g : 8 * g + 8, c * slots : (c + 1) * slots] for c in range(3)]
+            other = [
+                [cand[x, first + k, c, pl.ds(z + 1, 1), :] for c in range(3)] for k in chunk_ids
+            ]
+            found.append(pair_force(own, other))
+        found = [jnp.concatenate([f[c] for f in found], axis=0) for c in range(3)]
+        rounded = [f.astype(jnp.bfloat16) for f in found]
+        rest = [(f - r.astype(jnp.float32)).astype(jnp.bfloat16) for f, r in zip(found, rounded)]
+        sums = jnp.dot(
+            jnp.concatenate(rounded + rest, axis=1), summing, preferred_element_type=jnp.float32
+        )
+        for g, (x, _, _, rows, mask) in enumerate(work):
+            force_ref[x, rows, :] = force_ref[x, rows, :] + jnp.where(
+                mask, sums[8 * g : 8 * g + 8], 0.0
+            )
+        return carry
+
+    lax.fori_loop(0, steps, each_group, 0)
+
+
+def plane_kernel(
+    count_ref, own_ref, own_t, begun, filled_ref, box_ref, excess_ref, items, steps_ref,
+    reach, cand,
+):
+    _, ext_x, ext_z, slots = own_ref.shape
+    size_x, size_z = ext_x - 2, ext_z - 2
+    sides = cell_sides(slots)
+    letter = slots - 6
+    sub = lax.broadcasted_iota(jnp.int32, (ext_z, slots), 0)
+    lane = lax.broadcasted_iota(jnp.int32, (ext_z, slots), 1)
+    inner = (sub >= 1) & (sub <= size_z)
+    stayed = lane < letter - 1
+    far_tile = jnp.full((ext_z, slots), FAR, jnp.float32)
+
+    position = 0
+    for x in range(size_x):
+        for z in range(size_z):
+            code = x * 256 + z * 16
+            for block in range(slots // 8):
+                items[position + block] = code + block
+            position = position + lax.shift_right_logical(count_ref[x, 0, z] + 7, 3)
+    steps_ref[0] = lax.div(position + (GROUP - 1), GROUP)
+    for extra in range(GROUP):
+        items[position + extra] = slots // 8 - 1
+
+    lower, upper = [], []
+    for c in range(3):
+        low_tile = jnp.full((ext_z, slots), FAR, jnp.float32)
+        high_tile = jnp.full((ext_z, slots), -FAR, jnp.float32)
+        for x in range(1, size_x + 1):
+            tile = own_ref[c, x]
+            real = inner & stayed & (tile < NEAR)
+            low_tile = jnp.minimum(low_tile, jnp.where(real, tile, FAR))
+            high_tile = jnp.maximum(high_tile, jnp.where(real, tile, -FAR))
+        lower.append(jnp.min(low_tile, axis=(0, 1), keepdims=True) - (cut_radius + MARGIN))
+        upper.append(jnp.max(high_tile, axis=(0, 1), keepdims=True) + (cut_radius + MARGIN))
+        box_ref[c] = jnp.broadcast_to(lower[c], (ext_z, slots))
+        box_ref[3 + c] = jnp.broadcast_to(upper[c], (ext_z, slots))
+
+    centers = {}
+    from_z_low = (lane == letter + 4) & (sub > 0)
+    from_z_high = (lane == letter + 5) & (sub < ext_z - 1)
+    for x in range(ext_x):
+        settled = []
+        for c in range(3):
+            tile = own_ref[c, x]
+            out = jnp.where(stayed, tile, FAR)
+            if x > 0:
+                out = jnp.where(lane == letter, own_ref[c, x - 1], out)
+            if x < ext_x - 1:
+                out = jnp.where(lane == letter + 1, own_ref[c, x + 1], out)
+            out = jnp.where(from_z_low, pltpu.roll(tile, 1, 0), out)
+            settled.append(jnp.where(from_z_high, pltpu.roll(tile, ext_z - 1, 0), out))
+        centers[x] = settled
+        for dz in (-1, 0, 1):
+            tiles = settled
+            usable = inner
+            if dz:
+                tiles = [pltpu.roll(t, (-dz) % ext_z, 0) for t in tiles]
+                tiles[2] = tiles[2] + dz * sides[2]
+                usable = usable & ((tiles[2] > lower[2]) if dz < 0 else (tiles[2] < upper[2]))
+            reach[dz + 1, 0, x] = jnp.where(usable, tiles[0], FAR)
+            reach[dz + 1, 1, x] = tiles[1]
+            reach[dz + 1, 2, x] = tiles[2]
+
+    for x in range(size_x):
+        parts = []
+        rest = [jnp.where(stayed, own_ref[c, x + 1], FAR) for c in range(3)]
+        for _ in range(3):
+            rounded = [r.astype(jnp.bfloat16).astype(jnp.float32) for r in rest]
+            rest = [r - h for r, h in zip(rest, rounded)]
+            parts += rounded + [jnp.zeros((PART - 3 * ext_z, slots), jnp.float32)]
+        parts.append(jnp.zeros((slots - 3 * PART, slots), jnp.float32))
+        own_t[x] = jnp.concatenate(parts, axis=0).T
+
+    weights = scan_weights(slots)
+    excess = jnp.full((ext_z, slots), -1, jnp.int32)
+    for x in range(size_x):
+        count = jnp.zeros((ext_z, slots), jnp.int32)
+        for z in range(size_z):
+            count = jnp.where(sub == z + 1, count_ref[x, 0, z], count)
+        center = centers[x + 1]
+        sources = [(inner & (lane >= letter) & (center[0] < NEAR), center)]
+        for dx, _, dz in PLANE:
+            tiles = [reach[dz + 1, c, x + 1 + dx] for c in range(3)]
+            sources.append(sideways(tiles, dx, sides[0], lower[0], upper[0]))
+        chunks = [[jnp.where(lane < count, t, FAR) for t in center]]
+        chunks += [[far_tile] * 3 for _ in range(PLANE_CHUNKS - 1)]
+        chunks, filled, excess = append_sources(sources, chunks, count, excess, weights)
+        filled_ref[x] = jnp.maximum(filled - slots, 0)
+        for c in range(3):
+            cand[x, 0, c] = chunks[0][c]
+            for k in range(PLANE_CHUNKS - 1):
+                begun[x, k, c] = chunks[k + 1][c]
+    excess_ref[...] = excess
+    pair_loop(items, steps_ref[0], own_t, cand, (0,), own_t, slots, ext_z)
+
+
 def force_kernel(
     count_ref,
+    items,
+    steps_ref,
     own_ref,
     low_ref,
     high_ref,
     far_low_ref,
     far_high_ref,
     half_ref,
+    own_t,
+    begun,
+    filled_ref,
+    box_ref,
+    excess_ref,
     out_place_ref,
     out_velocity_ref,
     out_force_ref,
     comb,
     reach,
     cand,
-    own_t,
     force_t,
     arrival_force,
     chunk_count,
-    items,
     arrivals,
+    more_items,
 ):
     _, ext_x, ext_z, slots = own_ref.shape
     size_x, size_z = ext_x - 2, ext_z - 2
@@ -186,6 +379,8 @@
     inner = (sub >= 1) & (sub <= size_z)
     far_tile = jnp.full((ext_z, slots), FAR, jnp.float32)
     planes = [low_ref, own_ref, high_ref]
+    lower = [box_ref[c] for c in range(3)]
+    upper = [box_ref[3 + c] for c in range(3)]
 
     from_z_low = (lane == letter + 4) & (sub > 0)
     from_z_high = (lane == letter + 5) & (sub < ext_z - 1)
@@ -206,39 +401,30 @@
                 out = jnp.where(from_z_high, pltpu.roll(tile, ext_z - 1, 0), out)
                 comb[c, x, y] = out
 
-    lower, upper = [], []
-    for c in range(3):
-        low_tile = jnp.full((ext_z, slots), FAR, jnp.float32)
-        high_tile = jnp.full((ext_z, slots), -FAR, jnp.float32)
-        for x in range(1, size_x + 1):
-            tile = own_ref[c, x]
-            real = inner & (lane < letter - 1) & (tile < NEAR)
-            low_tile = jnp.minimum(low_tile, jnp.where(real, tile, FAR))
-            high_tile = jnp.maximum(high_tile, jnp.where(real, tile, -FAR))
-        lower.append(jnp.min(low_tile, axis=(0, 1), keepdims=True) - (cut_radius + MARGIN))
-        upper.append(jnp.max(high_tile, axis=(0, 1), keepdims=True) + (cut_radius + MARGIN))
-
+    spare = lane == letter - 2
     for x in range(ext_x):
-        for y in range(3):
+        for side, y in enumerate((0, 2)):
+            crossed = [
+                pltpu.roll(planes[y][c, x], slots - 4 - side, 1) for c in range(3)
+            ]
+            settled = [comb[c, x, y] for c in range(3)]
+            settled[1] = settled[1] + (y - 1) * sides[1]
+            settled = [jnp.where(spare, a, b) for a, b in zip(crossed, settled)]
+            reached = (settled[1] > lower[1]) if y == 0 else (settled[1] < upper[1])
+            settled[0] = jnp.where(reached, settled[0], FAR)
             for dz in (-1, 0, 1):
-                tiles = [comb[c, x, y] for c in range(3)]
+                tiles = settled
+                usable = inner
                 if dz:
                     tiles = [pltpu.roll(t, (-dz) % ext_z, 0) for t in tiles]
                     tiles[2] = tiles[2] + dz * sides[2]
-                usable = inner
-                if dz:
                     usable = usable & ((tiles[2] > lower[2]) if dz < 0 else (tiles[2] < upper[2]))
-                if y != 1:
-                    tiles[1] = tiles[1] + (y - 1) * sides[1]
-                    usable = usable & ((tiles[1] > lower[1]) if y == 0 else (tiles[1] < upper[1]))
-                reach[dz + 1, 0, x, y] = jnp.where(usable, tiles[0], FAR)
-                reach[dz + 1, 1, x, y] = tiles[1]
-                reach[dz + 1, 2, x, y] = tiles[2]
-
-    row_id = lax.broadcasted_iota(jnp.int32, (slots, 2 * slots), 0)
-    col_id = lax.broadcasted_iota(jnp.int32, (slots, 2 * slots), 1)
-    weights = jnp.where(row_id <= col_id, 1.0, 0.0).astype(jnp.bfloat16)
-    excess = jnp.full((ext_z, slots), -1, jnp.int32)
+                reach[dz + 1, 0, x, side] = jnp.where(usable, tiles[0], FAR)
+                reach[dz + 1, 1, x, side] = tiles[1]
+                reach[dz + 1, 2, x, side] = tiles[2]
+
+    weights = scan_weights(slots)
+    excess = excess_ref[...]
     counts = []
     for x in range(size_x):
         count = jnp.zeros((ext_z, slots), jnp.int32)
@@ -248,33 +434,13 @@
 
     chunk_tiles = []
     for x in range(size_x):
-        center = [comb[c, x + 1, 1] for c in range(3)]
-        sources = [(inner & (lane >= letter) & (center[0] < NEAR), center)]
-        for dx, dy, dz in NEIGHBOURS:
-            tiles = [reach[dz + 1, c, x + 1 + dx, 1 + dy] for c in range(3)]
-            real = tiles[0] < NEAR
-            if dx:
-                tiles[0] = tiles[0] + dx * sides[0]
-                real = real & ((tiles[0] > lower[0]) if dx < 0 else (tiles[0] < upper[0]))
-            sources.append((real, tiles))
-        masks = jnp.concatenate([jnp.where(m, 1.0, 0.0) for m, _ in sources], axis=0)
-        scanned = jnp.dot(
-            masks.astype(jnp.bfloat16), weights, preferred_element_type=jnp.float32
-        ).astype(jnp.int32)
-        split = []
-        for s in range(len(sources)):
-            part = scanned[ext_z * s : ext_z * (s + 1)]
-            split.append((part[:, :slots], part[:, slots:]))
-        chunks = [[jnp.where(lane < counts[x], t, FAR) for t in center]]
-        chunks += [[far_tile] * 3 for _ in range(CHUNKS - 1)]
-        filled = counts[x]
-        for batch in range(BATCHES):
-            ids = range(batch, len(sources), BATCHES)
-            chunks, filled, added = append_batch(
-                [sources[s][1] for s in ids], [split[s] for s in ids], chunks, filled
-            )
-            excess = jnp.maximum(excess, added - slots)
-        excess = jnp.maximum(excess, filled - CHUNKS * slots)
+        sources = []
+        for dx, dy, dz in SIDES:
+            tiles = [reach[dz + 1, c, x + 1 + dx, (dy + 1) // 2] for c in range(3)]
+            sources.append(sideways(tiles, dx, sides[0], lower[0], upper[0]))
+        chunks = [[begun[x, k, c] for c in range(3)] for k in range(PLANE_CHUNKS - 1)]
+        chunks += [[far_tile] * 3 for _ in range(CHUNKS - PLANE_CHUNKS + 1)]
+        chunks, filled, excess = append_sources(sources, chunks, filled_ref[x], excess, weights)
         for k in range(CHUNKS):
             for c in range(3):
                 cand[x, k, c] = chunks[k][c]
@@ -283,17 +449,9 @@
     overflow = jnp.max(excess.astype(jnp.float32)) > 0.0
     longest = functools.reduce(jnp.maximum, chunk_tiles)
     longest = jnp.max(jnp.where(inner, longest, 0).astype(jnp.float32)) > SHORT
-    position = 0
     for x in range(size_x):
         for z in range(size_z):
             chunk_count[x, z] = jnp.where(overflow, len(COMBOS), chunk_tiles[x][z + 1, 0])
-            code = x * 256 + z * 16
-            for block in range(slots // 8):
-                items[position + block] = code + block
-            position = position + lax.shift_right_logical(count_ref[x, 0, z] + 7, 3)
-    item_steps = lax.div(position + (GROUP - 1), GROUP)
-    for extra in range(GROUP):
-        items[position + extra] = slots // 8 - 1
     position = 0
     for x in range(size_x):
         arrived = jnp.zeros((ext_z, slots), jnp.float32)
@@ -319,65 +477,16 @@
                     if dz:
                         tile = pltpu.roll(tile, (-dz) % ext_z, 0)
                     cand[x, k, c] = tile + step * sides[c]
-
-    for x in range(size_x):
-        parts = []
-        rest = [comb[c, x + 1, 1] for c in range(3)]
-        for _ in range(3):
-            rounded = [r.astype(jnp.bfloat16).astype(jnp.float32) for r in rest]
-            rest = [r - h for r, h in zip(rest, rounded)]
-            parts += rounded + [jnp.zeros((PART - 3 * ext_z, slots), jnp.float32)]
-        parts.append(jnp.zeros((slots - 3 * PART, slots), jnp.float32))
-        own_t[x] = jnp.concatenate(parts, axis=0).T
+                    if k == 0:
+                        cand[x, len(COMBOS), c] = far_tile
+
+    for x in range(size_x):
         force_t[x] = jnp.zeros((slots, slots), jnp.float32)
-
     for x in range(size_x):
         for c in range(3):
             arrival_force[x, c] = jnp.zeros((ext_z, slots), jnp.float32)
 
-    row_id = lax.broadcasted_iota(jnp.int32, (slots, 3 * slots), 0)
-    col_id = lax.broadcasted_iota(jnp.int32, (slots, 3 * slots), 1)
-    of_axis = lax.shift_right_logical(row_id & (PART - 1), 3)
-    spread = (of_axis == lax.shift_right_logical(col_id, 7)) & (row_id < 3 * PART)
-    spread = jnp.where(spread, 1.0, 0.0).astype(jnp.bfloat16)
-    summing = jnp.ones((2 * slots, slots), jnp.bfloat16)
-
-    def each_group(group, carry):
-        work, held = [], []
-        for g in range(GROUP):
-            code = items[group * GROUP + g]
-            x = lax.shift_right_logical(code, 8)
-            z = lax.shift_right_logical(code, 4) & 15
-            rows = pl.ds(pl.multiple_of((code & 15) * 8, 8), 8)
-            held.append(jnp.where((lane & 7) == z + 1, own_t[x, rows, :], 0.0))
-            work.append((x, z, rows))
-        columns = jnp.dot(
-            jnp.concatenate(held, axis=0).astype(jnp.bfloat16),
-            spread,
-            preferred_element_type=jnp.float32,
-        )
-        found = []
-        for g, (x, z, _) in enumerate(work):
-            own = [columns[8 * g : 8 * g + 8, c * slots : (c + 1) * slots] for c in range(3)]
-            other = [
-                [cand[x, k, c, pl.ds(z + 1, 1), :] for c in range(3)] for k in range(SHORT)
-            ]
-            found += pair_force(own, other)
-        found = jnp.concatenate(found, axis=0)
-        rounded = found.astype(jnp.bfloat16)
-        rest = (found - rounded.astype(jnp.float32)).astype(jnp.bfloat16)
-        found = jnp.dot(
-            jnp.concatenate([rounded, rest], axis=1), summing, preferred_element_type=jnp.float32
-        )
-        for g, (x, z, rows) in enumerate(work):
-            result = force_t[x, rows, :]
-            for c in range(3):
-                start = (3 * g + c) * 8
-                result = jnp.where(lane == c * ext_z + z + 1, found[start : start + 8], result)
-            force_t[x, rows, :] = result
-        return carry
-
-    lax.fori_loop(0, item_steps, each_group, 0)
+    pair_loop(items, steps_ref[0], own_t, cand, range(SHORT), force_t, slots, ext_z)
 
     def each_arrival(group, carry):
         work = []
@@ -413,42 +522,34 @@
 
     lax.fori_loop(0, arrival_steps, each_arrival, 0)
 
-    lane_rows = lax.broadcasted_iota(jnp.int32, (ROWS, slots), 1)
-    row_shift = ROWS.bit_length() - 1
-
     @pl.when(overflow | longest)
     def _():
-        def each_x(x, carry):
-            for z in range(size_z):
-                picks = [c * ext_z + z + 1 for c in range(3)]
-                blocks = lax.shift_right_logical(count_ref[x, 0, z] + (ROWS - 1), row_shift)
-
-                def each_chunk(k, chunk_carry):
-                    def each_block(block, block_carry):
-                        rows = pl.ds(pl.multiple_of(block * ROWS, ROWS), ROWS)
-                        held = own_t[x, rows, :]
-                        own = []
-                        for p in picks:
-                            parts = [held[:, p + PART * i : p + PART * i + 1] for i in range(3)]
-                            own.append(parts[0] + parts[1] + parts[2])
-                        chunk = [cand[x, k, c, z + 1 : z + 2, :] for c in range(3)]
-                        found = row_sums(pair_force(own, [chunk]))
-                        result = force_t[x, rows, :]
-                        for c in range(3):
-                            result = jnp.where(lane_rows == picks[c], result + found[c], result)
-                        force_t[x, rows, :] = result
-                        return block_carry
-
-                    return lax.fori_loop(0, blocks, each_block, chunk_carry)
-
-                lax.fori_loop(SHORT, chunk_count[x, z], each_chunk, 0)
-            return carry
-
-        lax.fori_loop(0, size_x, each_x, 0)
-
+        def each_x(x, x_position):
+            def each_z(z, z_position):
+                blocks = lax.shift_right_logical(count_ref[x, 0, z] + 7, 3)
+
+                def each_part(part, part_position):
+                    def each_block(block, position):
+                        more_items[position] = part * (SHORT * 4096) + x * 256 + z * 16 + block
+                        return position + 1
+
+                    return lax.fori_loop(0, blocks, each_block, part_position)
+
+                parts = lax.div(chunk_count[x, z] + (SHORT - 1), SHORT)
+                return lax.fori_loop(1, parts, each_part, z_position)
+
+            return lax.fori_loop(0, size_z, each_z, x_position)
+
+        position = lax.fori_loop(0, size_x, each_x, 0)
+        for more in range(GROUP):
+            more_items[position + more] = slots // 8 - 1
+        steps = lax.div(position + (GROUP - 1), GROUP)
+        pair_loop(more_items, steps, own_t, cand, range(SHORT), force_t, slots, ext_z)
+
+    kept = jnp.where(overflow, 0.0, 1.0)
     speed = jnp.full((ext_z, slots), letter - 1, jnp.int32)
     for x in range(size_x):
-        turned = force_t[x].T
+        turned = (own_t[x] * kept + force_t[x]).T * 48.0
         count = counts[x]
         base = comb[0, x + 1, 1]
         filled = count
@@ -475,8 +576,9 @@
             for o in range(6):
                 half = jnp.where(lane == letter + o, take(sent[o], speed), half)
             where_to = placed if c == 0 else take(comb[c, x + 1, 1], index)
-            force = turned[c * ext_z : (c + 1) * ext_z]
-            force = jnp.where(lane >= letter, arrival_force[x, c], force)
+            start = 3 * PART + c * ext_z
+            force = turned[start : start + ext_z]
+            force = jnp.where(lane >= letter, arrival_force[x, c] * 48.0, force)
             force = jnp.where(alive, take(force, index), 0.0)
             half = take(half, index) + 0.5 * step_size * force
             where_to = jnp.where(alive, where_to, 0.0)
@@ -528,24 +630,45 @@
     far_high = far_low if lax.axis_size("gy") == 4 else shifted(letters, "gy", -2)
 
     ext_x, ext_z = size_x + 2, size_z + 2
+    room = size_x * size_z * (slots // 8) + GROUP
+    tile = (ext_z, slots)
+    params = pltpu.CompilerParams(vmem_limit_bytes=24 * 1024 * 1024)
+    own_t, begun, filled, box, excess, items, steps = pl.pallas_call(
+        plane_kernel,
+        out_shape=[
+            jax.ShapeDtypeStruct((size_x, slots, slots), jnp.float32),
+            jax.ShapeDtypeStruct((size_x, PLANE_CHUNKS - 1, 3) + tile, jnp.float32),
+            jax.ShapeDtypeStruct((size_x,) + tile, jnp.int32),
+            jax.ShapeDtypeStruct((6,) + tile, jnp.float32),
+            jax.ShapeDtypeStruct(tile, jnp.int32),
+            jax.ShapeDtypeStruct((room,), jnp.int32),
+            jax.ShapeDtypeStruct((1,), jnp.int32),
+        ],
+        in_specs=[smem, vmem],
+        out_specs=[vmem] * 5 + [smem] * 2,
+        scratch_shapes=[
+            pltpu.VMEM((3, 3, ext_x) + tile, jnp.float32),
+            pltpu.VMEM((size_x, 1, 3) + tile, jnp.float32),
+        ],
+        compiler_params=params,
+    )(counts, own)
     outs = pl.pallas_call(
         force_kernel,
         out_shape=[jax.ShapeDtypeStruct(swapped[0].shape, jnp.float32)] * 3,
-        in_specs=[smem] + [vmem] * 6,
+        in_specs=[smem] * 3 + [vmem] * 11,
         out_specs=[vmem] * 3,
         scratch_shapes=[
-            pltpu.VMEM((3, ext_x, 3, ext_z, slots), jnp.float32),
-            pltpu.VMEM((3, 3, ext_x, 3, ext_z, slots), jnp.float32),
-            pltpu.VMEM((size_x, len(COMBOS), 3, ext_z, slots), jnp.float32),
+            pltpu.VMEM((3, ext_x, 3) + tile, jnp.float32),
+            pltpu.VMEM((3, 3, ext_x, 2) + tile, jnp.float32),
+            pltpu.VMEM((size_x, len(COMBOS) + 1, 3) + tile, jnp.float32),
             pltpu.VMEM((size_x, slots, slots), jnp.float32),
-            pltpu.VMEM((size_x, slots, slots), jnp.float32),
-            pltpu.VMEM((size_x, 3, ext_z, slots), jnp.float32),
+            pltpu.VMEM((size_x, 3) + tile, jnp.float32),
             pltpu.SMEM((size_x, size_z), jnp.int32),
-            pltpu.SMEM((size_x * size_z * (slots // 8) + GROUP,), jnp.int32),
             pltpu.SMEM((size_x * size_z * 6 + ARRIVALS,), jnp.int32),
+            pltpu.SMEM((-(-len(COMBOS) // SHORT) * (room - GROUP) + GROUP,), jnp.int32),
         ],
-        compiler_params=pltpu.CompilerParams(vmem_limit_bytes=24 * 1024 * 1024),
-    )(counts, own, low, high, far_low, far_high, half)
+        compiler_params=params,
+    )(counts, items, steps, own, low, high, far_low, far_high, half, own_t, begun, filled, box, excess)
     return tuple(jnp.transpose(o, (0, 1, 3, 2, 4)) for o in outs)
 
 

time: 37.3 us -> 31.8 us (0.85)
  the two profiles are of different devices: /device:TPU:24 before, /device:TPU:0 now
where the time goes in v1:
time: 31.8 us; the launch traced here: 31.6 us
  Pallas kernels  17.8 us (56%)
  starting transfers between devices  8.93 us (28%)
  waiting for transfers between devices  3.16 us (10%)
  other arithmetic  0.9 us (3%)
  between operations  0.72 us (2%)
    pallas_call x1, Pallas kernels, per_device(): pl.pallas_call(force_kernel, out_shape=[jax.ShapeDtypeStruct(swapped[0].s...  9.85 us
    ppermute x6, starting transfers between devices, shifted(): lax.ppermute(value, axis, [(i, (i + steps) % count) for i in range(count)])  8.93 us
    pallas_call x1, Pallas kernels, per_device(): pl.pallas_call(plane_kernel, out_shape=[jax.ShapeDtypeStruct((size_x, slo...  6.19 us
    ppermute x6, waiting for transfers between devices, shifted(): lax.ppermute(value, axis, [(i, (i + steps) % count) for i in range(count)])  3.16 us
    pallas_call x1, Pallas kernels, per_device(): pl.pallas_call(pack_kernel, out_shape=[jax.ShapeDtypeStruct((4,) + flat,...  1.79 us
    concatenate x1, other arithmetic, per_device(): jnp.concatenate([slab[:, :1], slab[:, size_x - 1:]], axis=1)  0.85 us
  transfers between devices with their start and end apart: 6, of which 2 were waited for; matrix products, arithmetic and copies ran while one was open for 0% of the time, Pallas kernels for 20%

profile of v1, /device:TPU:0, one launch (start us, length us, event | category | flops | bytes accessed | tf_op | source)
XLA Modules:
  0.0 31.6 jit_solution(16769814680376127284)
XLA Ops:
  0.6 1.8 %shard_map.85 = (f32[4,6,6,128]{3,2,1,0:T(8,128)}, f32[4,6,1,128]{3,2,1,0:T(1,128)}, f32[4,6,1,128]{3,2,1,0:T(1,128)}, f32[3,6,6,128]{3,2,1,0:T(8,128)}) custom-call(s32[6,1,6]{2,1,0:T(1,128)} %count_ref.5, s32[16]{0:T(128)} %bitcast.13, s32[16]{0:T(128)} %bitcast.14, f32[3,6,6,1,128]{4,3,2,1,0:T(1,128)} %bitcast.10, f32[3,6,6,1,128]{4,3,2,1,0:T(1,128)} %bitcast.11, ...), custom_call_target="tpu_custom_call" | custom-call | tf_op jit(solution)/shard_map/pallas_call | solution.py:604
  2.4 3.0 %collective-permute-start = (f32[4,6,1,128]{3,2,1,0:T(1,128)}, f32[4,6,1,128]{3,2,1,0:T(1,128)S(1)}, u32[]{:S(2)}, u32[]{:S(2)}) collective-permute-start(f32[4,6,1,128]{3,2,1,0:T(1,128)} %get-tuple-element.17), channel_id=1, source_target_pairs={{0,1},{1,2},{2,3},{3,0},{4,5},{5,6},{6,7},{7,4},{8,9},{9,10},{10,1... | collective-permute-start | bytes 36872 | tf_op jit(solution)/shard_map/ppermute | solution.py:594
  5.4 2.1 %collective-permute-start.1 = (f32[4,6,1,128]{3,2,1,0:T(1,128)}, f32[4,6,1,128]{3,2,1,0:T(1,128)S(1)}, u32[]{:S(2)}, u32[]{:S(2)}) collective-permute-start(f32[4,6,1,128]{3,2,1,0:T(1,128)} %get-tuple-element.19), channel_id=1, source_target_pairs={{0,3},{1,0},{2,1},{3,2},{4,7},{5,4},{6,5},{7,6},{8,11},{9,8},{10,9... | collective-permute-start | bytes 36872 | tf_op jit(solution)/shard_map/ppermute | solution.py:594
  7.5 1.9 %collective-permute-done = f32[4,6,1,128]{3,2,1,0:T(1,128)S(1)} collective-permute-done((f32[4,6,1,128]{3,2,1,0:T(1,128)}, f32[4,6,1,128]{3,2,1,0:T(1,128)S(1)}, u32[]{:S(2)}, u32[]{:S(2)}) %collective-permute-start) | collective-permute-done | bytes 12320 | tf_op jit(solution)/shard_map/ppermute | solution.py:594
  9.5 0.0 collective-permute-done.1
  9.5 0.0 copy-start.2
  9.5 0.8 %fusion = f32[4,2,8,128]{3,2,1,0:T(8,128)S(1)} fusion(f32[4,6,1,128]{3,2,1,0:T(1,128)S(1)} %collective-permute-done.1, f32[4,6,6,128]{3,2,1,0:T(8,128)} %get-tuple-element.18, f32[4,6,1,128]{3,2,1,0:T(1,128)S(1)} %collective-permute-done), kind=kLoop, calls=%fused_computation.3 | loop fusion | flops 106496 | bytes 131072 | tf_op jit(solution)/shard_map/concatenate | solution.py:620
  10.3 0.1 collective-permute-start.2
  10.4 1.2 %collective-permute-done.2 = f32[4,2,8,128]{3,2,1,0:T(8,128)S(1)} collective-permute-done((f32[4,2,8,128]{3,2,1,0:T(8,128)S(1)}, f32[4,2,8,128]{3,2,1,0:T(8,128)S(1)}, u32[]{:S(2)}, u32[]{:S(2)}) %collective-permute-start.2) | collective-permute-done | bytes 32800 | tf_op jit(solution)/shard_map/ppermute | solution.py:594
  11.6 0.0 copy-done.2
  11.7 0.0 copy-start.1
  11.7 2.6 %collective-permute-start.4 = (f32[3,8,8,128]{3,2,1,0:T(8,128)S(1)}, f32[3,8,8,128]{3,2,1,0:T(8,128)S(1)}, u32[]{:S(2)}, u32[]{:S(2)}) collective-permute-start(f32[3,8,8,128]{3,2,1,0:T(8,128)S(1)} %slice.26.own_ref), channel_id=1, source_target_pairs={{0,12},{4,0},{8,4},{12,8},{1,13},{5,1},{9,5},{13,9},{2,14},{6,2},{... | collective-permute-start | bytes 294920 | tf_op jit(solution)/shard_map/ppermute | solution.py:594
  14.3 0.0 collective-permute-start.3
  14.3 0.0 copy-start
  14.3 1.2 %collective-permute-start.5 = (f32[8,8,128]{2,1,0:T(8,128)S(1)}, f32[8,8,128]{2,1,0:T(8,128)S(1)}, u32[]{:S(2)}, u32[]{:S(2)}) collective-permute-start(f32[8,8,128]{2,1,0:T(8,128)S(1)} %maximum_bitcast_fusion), channel_id=1, source_target_pairs={{0,8},{4,12},{8,0},{12,4},{1,9},{5,13},{9,1},{13,5},{2,10},{6,14},... | collective-permute-start | bytes 98312 | tf_op jit(solution)/shard_map/ppermute | solution.py:594
  15.5 0.0 copy-done.1
  15.5 6.2 %shard_map.86 = (f32[6,128,128]{2,1,0:T(8,128)S(1)}, f32[6,2,3,8,128]{4,3,2,1,0:T(8,128)S(1)}, s32[6,8,128]{2,1,0:T(8,128)S(1)}, f32[6,8,128]{2,1,0:T(8,128)S(1)...) custom-call(s32[6,1,6]{2,1,0:T(1,128)S(1)} %copy-done.1, f32[3,8,8,128]{3,2,1,0:T(8,128)S(1)} %slice.26.own_ref), custom_call_target="tpu_custom_call" | custom-call | tf_op jit(solution)/shard_map/pallas_call | solution.py:636
  21.7 0.0 collective-permute-done.5.far_low_ref.far_high_ref
  21.7 0.0 collective-permute-done.4.high_ref
  21.7 0.0 collective-permute-done.3.low_ref
  21.7 0.0 copy-done
  21.7 9.8 %shard_map.87 = (f32[3,6,6,1,128]{4,3,2,1,0:T(1,128)}, f32[3,6,6,1,128]{4,3,2,1,0:T(1,128)}, f32[3,6,6,1,128]{4,3,2,1,0:T(1,128)}) custom-call(s32[6,1,6]{2,1,0:T(1,128)S(1)} %copy-done.1, s32[624]{0:T(1024)S(1)} %get-tuple-element.20.items, s32[1]{0:T(128)} %get-tuple-element.21.steps_ref, f32[3,8,8,128]{3,2,1,0:T(8,128)S(1)} %slice.26.own_ref, ...), custom_call_target="tpu_custom_call" | custom-call | tf_op jit(solution)/shard_map/pallas_call | solution.py:655
  (4 shorter events, 0.1 us)
Async XLA Ops:
  2.4 7.0 %collective-permute-start = (f32[4,6,1,128]{3,2,1,0:T(1,128)}, f32[4,6,1,128]{3,2,1,0:T(1,128)S(1)}, u32[]{:S(2)}, u32[]{:S(2)}) collective-permute-start(f32[4,6,1,128]{3,2,1,0:T(1,128)} %get-tuple-element.17), channel_id=1, source_target_pairs={{0,1},{1,2},{2,3},{3,0},{4,5},{5,6},{6,7},{7,4},{8,9},{9,10},{10,1... | collective-permute-start | bytes 36872 | tf_op jit(solution)/shard_map/ppermute | solution.py:594
  5.4 4.0 %collective-permute-start.1 = (f32[4,6,1,128]{3,2,1,0:T(1,128)}, f32[4,6,1,128]{3,2,1,0:T(1,128)S(1)}, u32[]{:S(2)}, u32[]{:S(2)}) collective-permute-start(f32[4,6,1,128]{3,2,1,0:T(1,128)} %get-tuple-element.19), channel_id=1, source_target_pairs={{0,3},{1,0},{2,1},{3,2},{4,7},{5,4},{6,5},{7,6},{8,11},{9,8},{10,9... | collective-permute-start | bytes 36872 | tf_op jit(solution)/shard_map/ppermute | solution.py:594
  9.5 2.1 %copy-start.2 = (f32[4,6,6,128]{3,2,1,0:T(8,128)S(1)}, f32[4,6,6,128]{3,2,1,0:T(8,128)}, u32[]{:S(2)}) copy-start(f32[4,6,6,128]{3,2,1,0:T(8,128)} %get-tuple-element.18) | copy-start | bytes 221188
  10.3 1.3 %collective-permute-start.2 = (f32[4,2,8,128]{3,2,1,0:T(8,128)S(1)}, f32[4,2,8,128]{3,2,1,0:T(8,128)S(1)}, u32[]{:S(2)}, u32[]{:S(2)}) collective-permute-start(f32[4,2,8,128]{3,2,1,0:T(8,128)S(1)} %fusion), channel_id=1, source_target_pairs={{0,16},{16,0},{1,17},{17,1},{2,18},{18,2},{3,19},{19,3},{4,20},{20... | collective-permute-start | bytes 98312 | tf_op jit(solution)/shard_map/ppermute | solution.py:594
  11.7 3.8 %copy-start.1 = (s32[6,1,6]{2,1,0:T(1,128)S(1)}, s32[6,1,6]{2,1,0:T(1,128)}, u32[]{:S(2)}) copy-start(s32[6,1,6]{2,1,0:T(1,128)} %count_ref.5) | copy-start | bytes 436
  11.7 10.0 %collective-permute-start.4 = (f32[3,8,8,128]{3,2,1,0:T(8,128)S(1)}, f32[3,8,8,128]{3,2,1,0:T(8,128)S(1)}, u32[]{:S(2)}, u32[]{:S(2)}) collective-permute-start(f32[3,8,8,128]{3,2,1,0:T(8,128)S(1)} %slice.26.own_ref), channel_id=1, source_target_pairs={{0,12},{4,0},{8,4},{12,8},{1,13},{5,1},{9,5},{13,9},{2,14},{6,2},{... | collective-permute-start | bytes 294920 | tf_op jit(solution)/shard_map/ppermute | solution.py:594
  14.3 7.4 %collective-permute-start.3 = (f32[3,8,8,128]{3,2,1,0:T(8,128)S(1)}, f32[3,8,8,128]{3,2,1,0:T(8,128)S(1)}, u32[]{:S(2)}, u32[]{:S(2)}) collective-permute-start(f32[3,8,8,128]{3,2,1,0:T(8,128)S(1)} %slice.26.own_ref), channel_id=1, source_target_pairs={{0,4},{4,8},{8,12},{12,0},{1,5},{5,9},{9,13},{13,1},{2,6},{6,10},{... | collective-permute-start | bytes 294920 | tf_op jit(solution)/shard_map/ppermute | solution.py:594
  14.3 7.4 %copy-start = (f32[3,6,6,128]{3,2,1,0:T(8,128)S(1)}, f32[3,6,6,128]{3,2,1,0:T(8,128)}, u32[]{:S(2)}) copy-start(f32[3,6,6,128]{3,2,1,0:T(8,128)} %get-tuple-element.22.half_ref) | copy-start | bytes 165892
  14.3 7.4 %collective-permute-start.5 = (f32[8,8,128]{2,1,0:T(8,128)S(1)}, f32[8,8,128]{2,1,0:T(8,128)S(1)}, u32[]{:S(2)}, u32[]{:S(2)}) collective-permute-start(f32[8,8,128]{2,1,0:T(8,128)S(1)} %maximum_bitcast_fusion), channel_id=1, source_target_pairs={{0,8},{4,12},{8,0},{12,4},{1,9},{5,13},{9,1},{13,5},{2,10},{6,14},... | collective-permute-start | bytes 98312 | tf_op jit(solution)/shard_map/ppermute | solution.py:594
